TPU v7x, 32 devices: a whole 2x2x4 slice. The times are simulated.
32 devices in a mesh: group: 2 (over y), expert: 2 (over core), tensor: 8 (over z, x).
Axes of the slice: x: 2, y: 2, z: 4, core: 2. Of those that a mesh axis runs over, the one named last changes fastest.
Arguments:
- tokens: bfloat16 [512, 6144], P(('group', 'expert'), 'tensor'), parts along dimension 0, may hold values from -6 to 6
- routes: int32 [512, 2], P('group'), parts along dimension 0, may hold values from 0 to 3, all different within a row; in each aligned block of 128 rows (0 to 127, 128 to 255, ...) at most 128 rows name the same one
- route_weights: float32 [512, 2], P('group'), parts along dimension 0, may hold values from 0.1 to 0.9
- gate_weight: bfloat16 [4, 8192, 6144], P('expert', 'tensor'), may hold values from -0.078125 to 0.078125
- up_weight: bfloat16 [4, 8192, 6144], P('expert', 'tensor'), may hold values from -0.078125 to 0.078125
- down_weight: bfloat16 [4, 6144, 8192], P('expert', 'tensor'), may hold values from -0.0625 to 0.0625
Outputs:
- mixed: bfloat16 [512, 6144], P(('group', 'expert'), 'tensor'), parts along dimension 0
There are 2 independent parts, one for each index of `group`. A program takes and returns all parts, laid end to end along the dimension named above; an argument that names none is the same for every part. Nothing has to cross between parts.
Inputs may be any that keep to these rules, and one draw needn't show every extreme that they name: `routes`: each row names two different experts.
All inputs are finite; a program needn't handle non-finite values.
Results may differ from a plain program's by a relative error of at most 0.005.
Values may be sent and summed in bfloat16 or wider, within the bound.
A program may use at most 192 MiB of HBM per device.

v0:
```python
import jax
import jax.numpy as jnp
from jax import lax
from jax.sharding import PartitionSpec as P


def positions(block_routes, experts, capacity):
    hits = (block_routes[:, :, None] == jnp.arange(experts, dtype=jnp.int32)[None, None, :]).astype(
        jnp.int32
    )
    per_token = jnp.sum(hits, axis=1)
    before = jnp.cumsum(per_token, axis=0) - per_token
    slot = jnp.sum(hits * before[:, None, :], axis=2)
    return block_routes * capacity + slot


def shards(tokens, routes, route_weights, gate_weight, up_weight, down_weight):
    exp_dev = gate_weight.shape[0]
    owners = lax.axis_size("expert")
    experts = exp_dev * owners
    rows = routes.shape[0] // owners
    slots_all = experts * rows
    owner_id = lax.axis_index("expert")
    blocks = routes.reshape(owners, rows, 2)
    flat = jax.vmap(positions, (0, None, None))(blocks, experts, rows)
    own_flat = lax.dynamic_index_in_dim(flat, owner_id, 0, keepdims=False)
    slot_ids = jnp.arange(slots_all, dtype=jnp.int32)
    picker = jnp.sum(
        (slot_ids[:, None, None] == own_flat[None, :, :]).astype(jnp.float32), axis=2
    ).astype(jnp.bfloat16)
    features = lax.all_gather(tokens, "tensor", axis=1, tiled=True)
    packed = jnp.dot(picker, features, preferred_element_type=jnp.float32).astype(jnp.bfloat16)
    packed = packed.reshape(owners, exp_dev, rows, features.shape[1])
    arrived = lax.all_to_all(packed, "expert", split_axis=0, concat_axis=2, tiled=True)[0]
    gate = jnp.einsum("esd,ehd->esh", arrived, gate_weight, preferred_element_type=jnp.float32)
    up = jnp.einsum("esd,ehd->esh", arrived, up_weight, preferred_element_type=jnp.float32)
    hidden = (jax.nn.silu(gate) * up).astype(jnp.bfloat16)
    d_local = down_weight.shape[1]
    result = jnp.einsum(
        "esf,edf->esd",
        lax.all_gather(hidden, "tensor", axis=2, tiled=True),
        down_weight,
        preferred_element_type=jnp.float32,
    )
    weight_blocks = route_weights.reshape(owners, rows, 2)
    matches = slot_ids[None, None, :, None] == flat[:, :, None, :]
    mixer_all = jnp.sum(jnp.where(matches, weight_blocks[:, :, None, :], jnp.float32(0.0)), axis=3)
    parts = result.reshape(exp_dev, owners, rows, d_local)
    returned = lax.all_to_all(parts, "expert", split_axis=1, concat_axis=0, tiled=True)
    mixer = lax.dynamic_index_in_dim(mixer_all, owner_id, 0, keepdims=False)
    mixed = jnp.dot(
        mixer,
        returned.reshape(slots_all, d_local),
        precision=lax.Precision.HIGHEST,
        preferred_element_type=jnp.float32,
    )
    return mixed.astype(jnp.bfloat16)


def solution(mesh):
    placed = (
        P(("group", "expert"), "tensor"),
        P("group", None),
        P("group", None),
        P("expert", "tensor", None),
        P("expert", "tensor", None),
        P("expert", "tensor", None),
    )
    return jax.shard_map(
        shards,
        mesh=mesh,
        in_specs=placed,
        out_specs=P(("group", "expert"), "tensor"),
        check_vma=False,
    )
```

profile of v0, /device:TPU:0, one launch (start us, length us, event | category | flops | bytes accessed | tf_op | source)
XLA Modules:
  0.0 250.5 jit_solution(5251790429608511340)
XLA Ops:
  6.5 0.0 all-gather.3.cloned.1.call-start
  6.5 0.7 all-gather.3.cloned.1.call-update
  7.3 0.0 all-gather.5.cloned.1.call-start
  7.3 0.7 convert_reduce_fusion.1
  8.0 0.1 copy.18
  8.1 0.2 reduce_window_sum.11
  8.4 0.1 copy.20
  8.4 0.7 select_reduce_fusion.1
  9.2 0.7 multiply_add_fusion
  9.8 0.1 convert_reduce_fusion
  9.9 46.8 %all-gather.3.cloned.1.call-done = bf16[128,6144]{1,0:T(8,128)(2,1)} async-done(((bf16[128,768]{1,0:T(8,128)(2,1)}), bf16[128,6144]{1,0:T(8,128)(2,1)}) %all-gather.3.cloned.1.call-update) | async-done | bytes 1572880 | tf_op jit(solution)/shard_map/all_gather | solution.py:31
  56.7 3.2 %convolution_convert_fusion = bf16[512,6144]{1,0:T(8,128)(2,1)S(1)} fusion(bf16[128,6144]{1,0:T(8,128)(2,1)} %all-gather.3.cloned.1.call-done, bf16[512,128]{1,0:T(8,128)(2,1)S(1)} %convert_reduce_fusion), kind=kOutput, calls=%fused_computation | convolution fusion | flops 808452096 | bytes 7995392 | tf_op jit(solution)/shard_map/dot_general | solution.py:32
  59.9 8.8 %all_to_all.30 = bf16[2,2,128,6144]{3,2,1,0:T(8,128)(2,1)S(1)} all-to-all(bf16[2,2,128,6144]{3,2,1,0:T(8,128)(2,1)S(1)} %bitcast.28), channel_id=1, replica_groups=mesh['group'=2,'expert'=2,'tensor'=8] {'expert'}, dimensions={0} | all-to-all | bytes 12582912 | tf_op jit(solution)/shard_map/all_to_all | solution.py:34
  68.7 3.1 %copy.22 = bf16[1,2,2,128,6144]{4,3,2,1,0:T(8,128)(2,1)} copy(bf16[1,2,2,128,6144]{4,3,1,2,0:T(8,128)(2,1)S(1)} %bitcast.29) | data formatting | bytes 12582912 | tf_op jit(solution)/shard_map/all_to_all | solution.py:34
  71.8 13.1 %fusion.4 = f32[2,256,1024]{2,1,0:T(8,128)S(1)} fusion(bf16[2,256,6144]{2,1,0:T(8,128)(2,1)} %bitcast.30, bf16[2,1024,6144]{2,1,0:T(8,128)(2,1)} %param.9), kind=kOutput, calls=%fused_computation.16 | convolution fusion | flops 6442450944 | bytes 33554432 | tf_op jit(solution)/shard_map/esd,ehd->esh/dot_general | solution.py:35
  85.0 0.0 copy-start
  85.0 14.4 %multiply_convert_fusion = bf16[2,256,1024]{2,1,0:T(8,128)(2,1)} fusion(f32[2,256,1024]{2,1,0:T(8,128)S(1)} %fusion.4, bf16[2,256,6144]{2,1,0:T(8,128)(2,1)} %bitcast.31, bf16[2,1024,6144]{2,1,0:T(8,128)(2,1)} %param.10), kind=kOutput, calls=%fused_computation.1 | convolution fusion | flops 6445596672 | bytes 34603008 | tf_op jit(solution)/shard_map/esd,ehd->esh/dot_general | solution.py:36
  99.4 0.0 all-gather.5.cloned.1.call-update
  99.4 0.0 copy-done
  99.5 0.2 select_reduce_fusion
  99.7 123.3 %all-gather.5.cloned.1.call-done = bf16[2,256,8192]{2,1,0:T(8,128)(2,1)} async-done(((bf16[2,256,1024]{2,1,0:T(8,128)(2,1)}), bf16[2,256,8192]{2,1,0:T(8,128)(2,1)}) %all-gather.5.cloned.1.call-update) | async-done | bytes 8388624 | tf_op jit(solution)/shard_map/all_gather | solution.py:41
  223.0 13.9 %fusion.5 = f32[2,256,768]{2,1,0:T(8,128)S(1)} fusion(bf16[2,256,8192]{2,1,0:T(8,128)(2,1)} %all-gather.5.cloned.1.call-done, bf16[2,768,8192]{2,1,0:T(8,128)(2,1)} %param.11), kind=kOutput, calls=%fused_computation.17 | convolution fusion | flops 6442450944 | bytes 35127296 | tf_op jit(solution)/shard_map/esf,edf->esd/dot_general | solution.py:39
  236.9 0.1 copy.23
  237.0 5.0 %all_to_all.31 = f32[2,2,128,768]{3,2,0,1:T(8,128)S(1)} all-to-all(f32[2,2,128,768]{3,2,0,1:T(8,128)S(1)} %copy.23), channel_id=1, replica_groups=mesh['group'=2,'expert'=2,'tensor'=8] {'expert'}, dimensions={1} | all-to-all | bytes 3145728 | tf_op jit(solution)/shard_map/all_to_all | solution.py:49
  242.0 1.7 convolution_convert_fusion.1
  (2 shorter events, 0.0 us)
Async XLA Ops:
  6.5 50.2 %all-gather.3.cloned.1.call-start = ((), (), s32[]{:S(2)}) async-start(), calls=%async_computation.2 | async-start | bytes 1769472 | tf_op jit(solution)/shard_map/all_gather | solution.py:31
  7.3 215.7 %all-gather.5.cloned.1.call-start = ((), (), s32[]{:S(2)}) async-start(), calls=%async_computation.3 | async-start | bytes 9437184 | tf_op jit(solution)/shard_map/all_gather | solution.py:41
  85.0 14.5 %copy-start = (f32[256,2]{0,1:T(2,128)S(1)}, f32[256,2]{0,1:T(2,128)}, u32[]{:S(2)}) copy-start(f32[256,2]{0,1:T(2,128)} %param.8) | copy-start | bytes 6148
Sparse Core Ops, SparseCore 0:
  9.6 47.1 all-gather.2
  99.6 123.3 all-gather.4
where the time goes:
time: 251 us
  waiting for transfers between devices  171 us (68%)
  matrix products  46.4 us (18%)
  blocking collectives  13.8 us (5%)
  between operations  13.5 us (5%)
  local copies, waits for them, and re-layouts  3.41 us (1%)
  other arithmetic  2.58 us (1%)
    all_gather x1, waiting for transfers between devices, shards(): lax.all_gather(hidden, 'tensor', axis=2, tiled=True)  123 us
    all_gather x1, waiting for transfers between devices, shards(): features = lax.all_gather(tokens, 'tensor', axis=1, tiled=True)  46.8 us
    dot_general x1, matrix products, shards(): jnp.einsum('esd,ehd->esh', arrived, up_weight, preferred_element_type=jnp...  14.4 us
    dot_general x1, matrix products, shards(): jnp.einsum('esf,edf->esd', lax.all_gather(hidden, 'tensor', axis=2, tiled...  13.9 us
    dot_general x1, matrix products, shards(): jnp.einsum('esd,ehd->esh', arrived, gate_weight, preferred_element_type=j...  13.1 us
    all_to_all x1, blocking collectives, shards(): lax.all_to_all(packed, 'expert', split_axis=0, concat_axis=2, tiled=True)[0]  8.79 us
  transfers between devices with their start and end apart: 2, of which 2 were waited for; matrix products, arithmetic and copies ran while one was open for 1% of the time, Pallas kernels for 0%

commit v1 on v0

--- a/solution.py
+++ b/solution.py
@@ -1,7 +1,15 @@
+import functools
 import jax
 import jax.numpy as jnp
 from jax import lax
+from jax.experimental import pallas as pl
+from jax.experimental.pallas import tpu as pltpu
 from jax.sharding import PartitionSpec as P
+
+MESH = pl.DeviceIdType.MESH
+F32 = jnp.float32
+BF16 = jnp.bfloat16
+SLOTS = 3
 
 
 def positions(block_routes, experts, capacity):
@@ -14,7 +22,7 @@
     return block_routes * capacity + slot
 
 
-def shards(tokens, routes, route_weights, gate_weight, up_weight, down_weight):
+def general(tokens, routes, route_weights, gate_weight, up_weight, down_weight):
     exp_dev = gate_weight.shape[0]
     owners = lax.axis_size("expert")
     experts = exp_dev * owners
@@ -57,6 +65,284 @@
     return mixed.astype(jnp.bfloat16)
 
 
+def dot_t(a, b):
+    return lax.dot_general(a, b, (((1,), (1,)), ((), ())), preferred_element_type=F32)
+
+
+def ring_kernel(
+    tok_ref, routes_ref, rw_ref, gate_ref, up_ref, down_ref, out_ref,
+    xbuf, wbuf, dbuf, acc, hbuf, sown, pbuf, qbuf, sbuf, racc, cbuf, ebuf,
+    wsem, dsem, ring_send, ring_recv, sis_send, sis_recv, pq_send, pq_recv, fin_send, fin_recv,
+):
+    g = lax.axis_index("group")
+    c = lax.axis_index("expert")
+    t = lax.axis_index("tensor")
+    n = 8
+    half = n // 2
+    dl = tok_ref.shape[1]
+    ul = gate_ref.shape[1]
+    uh = ul // 2
+    rows = routes_ref.shape[0]
+
+    tx = t % 2
+    pos = (t // 2) * (1 - tx) + (n - 1 - t // 2) * tx
+
+    def tid(p):
+        p = (p + n) % n
+        px = p // half
+        return 2 * (p * (1 - px) + (n - 1 - p) * px) + px
+
+    def origin(seq):
+        if seq == 0:
+            return tid(pos)
+        d = (seq + 1) // 2
+        return tid(pos - d if seq % 2 else pos + d)
+
+    right, left = tid(pos + 1), tid(pos - 1)
+    to = ((g, c, right), (g, c, left))
+    sister = (g, 1 - c, t)
+
+    def seq_of(way, d):
+        return n - 1 if d == half else 2 * d - 1 + way
+
+    def w_copies(seq):
+        cols = pl.ds(pl.multiple_of(origin(seq) * dl, 128), dl)
+        s = seq % SLOTS
+        return [
+            pltpu.make_async_copy(ref.at[:, :, cols], wbuf.at[s, i], wsem.at[s, i])
+            for i, ref in enumerate((gate_ref, up_ref))
+        ]
+
+    def d_copy(seq):
+        cols = pl.ds(pl.multiple_of(origin(seq) * ul, 128), ul)
+        return pltpu.make_async_copy(down_ref.at[:, :, cols], dbuf.at[seq], dsem.at[seq])
+
+    for seq in range(SLOTS):
+        for cp in w_copies(seq):
+            cp.start()
+
+    xbuf[0, pl.ds(c, 1)] = tok_ref[...].reshape(1, 2, rows // 4, dl)
+
+    barrier = pltpu.get_barrier_semaphore()
+    for dev in (to[0], to[1], sister):
+        pl.semaphore_signal(barrier, inc=1, device_id=dev, device_id_type=MESH)
+    pl.semaphore_wait(barrier, 3)
+
+    def place(phase, seq, h):
+        if phase == 0:
+            return xbuf.at[seq, c, h]
+        return sown.at[h] if seq == 0 else sbuf.at[seq - 1, c, h]
+
+    def ring_copy(phase, way, d, h):
+        src = place(phase, 0 if d == 1 else seq_of(way, d - 1), h)
+        return pltpu.make_async_remote_copy(
+            src_ref=src, dst_ref=place(phase, seq_of(way, d), h),
+            send_sem=ring_send.at[phase, way, d - 1, h], recv_sem=ring_recv.at[phase, way, d - 1, h],
+            device_id=to[way], device_id_type=MESH,
+        )
+
+    def sis_copy(phase, seq, h):
+        ref = place(phase, seq, h)
+        return pltpu.make_async_remote_copy(
+            src_ref=ref, dst_ref=ref,
+            send_sem=sis_send.at[phase, seq, h], recv_sem=sis_recv.at[phase, seq, h],
+            device_id=sister, device_id_type=MESH,
+        )
+
+    def sis_wait(phase, seq, h):
+        ref = xbuf.at[seq, 1 - c, h] if phase == 0 else sbuf.at[seq - 1, 1 - c, h]
+        pltpu.make_async_remote_copy(
+            src_ref=ref, dst_ref=ref,
+            send_sem=sis_send.at[phase, seq, h], recv_sem=sis_recv.at[phase, seq, h],
+            device_id=sister, device_id_type=MESH,
+        ).wait_recv()
+
+    pending = []
+
+    def start(cp):
+        cp.start()
+        pending.append(cp)
+
+    def travels(d, way, h):
+        return d < half or (d == half and h == way)
+
+    def arrive(phase, d, h, way):
+        ring_copy(phase, way, d, h).wait_recv()
+        if d < half and travels(d + 1, way, h):
+            start(ring_copy(phase, way, d + 1, h))
+        start(sis_copy(phase, seq_of(way, d), h))
+
+    def gate_up_half(seq, h):
+        s = seq % SLOTS
+
+        def body(i, carry):
+            gu, e = i // 2, i % 2
+            x = xbuf[seq].reshape(rows, dl)
+            r = dot_t(x, wbuf[s, gu, e, h * uh:(h + 1) * uh, :])
+            if seq == 0:
+                acc[gu, e, h] = r
+            else:
+                acc[gu, e, h] += r
+            return carry
+
+        lax.fori_loop(0, 4, body, 0)
+
+    def w_wait(seq):
+        for cp in w_copies(seq):
+            cp.wait()
+
+    def gate_up(seq):
+        for h in range(2):
+            sis_wait(0, seq, h)
+        w_wait(seq)
+        for h in range(2):
+            gate_up_half(seq, h)
+        if seq + SLOTS < n:
+            for cp in w_copies(seq + SLOTS):
+                cp.start()
+        if seq + SLOTS == n - 1:
+            for q in range(n):
+                d_copy(q).start()
+
+    for h in range(2):
+        for way in range(2):
+            start(ring_copy(0, way, 1, h))
+        start(sis_copy(0, 0, h))
+    gate_up(0)
+    for d in range(1, half):
+        for h in range(2):
+            for way in range(2):
+                arrive(0, d, h, way)
+        for way in range(2):
+            gate_up(seq_of(way, d))
+    for h in range(2):
+        arrive(0, half, h, h)
+    for h in range(2):
+        sis_wait(0, n - 1, h)
+    w_wait(n - 1)
+
+    r0, r1 = routes_ref[:, 0:1], routes_ref[:, 1:2]
+    mine = jnp.where(c == 0, r0, r1)
+    other = jnp.where(c == 0, r1, r0)
+
+    def hidden(h):
+        hs = []
+        for e in range(2):
+            v = acc[0, e, h]
+            hs.append(v / (1.0 + jnp.exp(-v)) * acc[1, e, h])
+        pbuf[h] = jnp.where(other == 2 * c, hs[0], hs[1]).astype(BF16)
+        sown[h] = jnp.where(mine == 2 * c, hs[0], hs[1]).astype(BF16)
+        for e in range(2):
+            hbuf[e, h] = hs[e].astype(BF16)
+
+    def pq_copy(h):
+        return pltpu.make_async_remote_copy(
+            src_ref=pbuf.at[h], dst_ref=qbuf.at[h], send_sem=pq_send.at[h], recv_sem=pq_recv.at[h],
+            device_id=sister, device_id_type=MESH,
+        )
+
+    def merge(h):
+        pq_copy(h).wait_recv()
+        sown[h] = jnp.where(mine // 2 == c, sown[h].astype(F32), qbuf[h].astype(F32)).astype(BF16)
+        for way in range(2):
+            start(ring_copy(1, way, 1, h))
+
+    def down(seq, h):
+        def body(e, carry):
+            if seq == 0:
+                a = hbuf[e, h]
+            else:
+                a = jnp.where(r0 == 2 * c + e, sbuf[seq - 1, 0, h].astype(F32), sbuf[seq - 1, 1, h].astype(F32)).astype(BF16)
+            r = dot_t(a, dbuf[seq, e, :, h * uh:(h + 1) * uh])
+            if seq == 0 and h == 0:
+                racc[e] = r
+            else:
+                racc[e] += r
+            return carry
+
+        lax.fori_loop(0, 2, body, 0)
+
+    gate_up_half(n - 1, 0)
+    hidden(0)
+    start(pq_copy(0))
+    gate_up_half(n - 1, 1)
+    merge(0)
+    hidden(1)
+    start(pq_copy(1))
+    d_copy(0).wait()
+    down(0, 0)
+    merge(1)
+    down(0, 1)
+    for d in range(1, half + 1):
+        for h in range(2):
+            ways = [way for way in range(2) if travels(d, way, h)]
+            for way in ways:
+                arrive(1, d, h, way)
+            for way in ways:
+                seq = seq_of(way, d)
+                if h == 0:
+                    d_copy(seq).wait()
+                sis_wait(1, seq, h)
+                down(seq, h)
+
+    w0, w1 = rw_ref[:, 0:1], rw_ref[:, 1:2]
+    zero = jnp.zeros_like(w0)
+    total = None
+    for e in range(2):
+        f = jnp.where(r0 == 2 * c + e, w0, zero) + jnp.where(r1 == 2 * c + e, w1, zero)
+        term = f * racc[e]
+        total = term if total is None else total + term
+    cbuf[...] = total.reshape(2, rows // 2, dl)
+    fin = pltpu.make_async_remote_copy(
+        src_ref=cbuf.at[1 - c], dst_ref=ebuf, send_sem=fin_send, recv_sem=fin_recv,
+        device_id=sister, device_id_type=MESH,
+    )
+    start(fin)
+    fin.wait_recv()
+    out_ref[...] = (cbuf[c] + ebuf[...]).astype(BF16)
+    for cp in pending:
+        cp.wait_send()
+
+
+def fused(tokens, routes, route_weights, gate_weight, up_weight, down_weight):
+    n = 8
+    rows, dl = routes.shape[0], tokens.shape[1]
+    ul, uh = gate_weight.shape[1], gate_weight.shape[1] // 2
+    vmem = pl.BlockSpec(memory_space=pltpu.VMEM)
+    hbm = pl.BlockSpec(memory_space=pl.ANY)
+    dma = pltpu.SemaphoreType.DMA
+    flops = 2 * 2 * rows * ul * dl * n * 3
+    moved = 2 * (gate_weight.size + up_weight.size + down_weight.size)
+    return pl.pallas_call(
+        ring_kernel,
+        out_shape=jax.ShapeDtypeStruct(tokens.shape, BF16),
+        in_specs=[vmem, vmem, vmem, hbm, hbm, hbm],
+        out_specs=vmem,
+        scratch_shapes=[
+            pltpu.VMEM((n, 2, 2, rows // 4, dl), BF16),
+            pltpu.VMEM((SLOTS, 2, 2, ul, dl), BF16),
+            pltpu.VMEM((n, 2, dl, ul), BF16),
+            pltpu.VMEM((2, 2, 2, rows, uh), F32),
+            pltpu.VMEM((2, 2, rows, uh), BF16),
+            pltpu.VMEM((2, rows, uh), BF16),
+            pltpu.VMEM((2, rows, uh), BF16),
+            pltpu.VMEM((2, rows, uh), BF16),
+            pltpu.VMEM((n - 1, 2, 2, rows, uh), BF16),
+            pltpu.VMEM((2, rows, dl), F32),
+            pltpu.VMEM((2, rows // 2, dl), F32),
+            pltpu.VMEM((rows // 2, dl), F32),
+            dma((SLOTS, 2)), dma((n,)),
+            dma((2, 2, n // 2, 2)), dma((2, 2, n // 2, 2)),
+            dma((2, n, 2)), dma((2, n, 2)),
+            dma((2,)), dma((2,)), dma, dma,
+        ],
+        compiler_params=pltpu.CompilerParams(
+            collective_id=0, has_side_effects=True, vmem_limit_bytes=64 * 1024 * 1024 - 256 * 1024
+        ),
+        cost_estimate=pl.CostEstimate(flops=flops, bytes_accessed=moved, transcendentals=4 * rows * ul),
+    )(tokens, routes, route_weights, gate_weight, up_weight, down_weight)
+
+
 def solution(mesh):
     placed = (
         P(("group", "expert"), "tensor"),
@@ -66,8 +352,9 @@
         P("expert", "tensor", None),
         P("expert", "tensor", None),
     )
+    fits = mesh.shape["tensor"] == 8 and mesh.shape["expert"] == 2
     return jax.shard_map(
-        shards,
+        fused if fits else general,
         mesh=mesh,
         in_specs=placed,
         out_specs=P(("group", "expert"), "tensor"),

time: 251 us -> 93 us (0.37)
  waiting for transfers between devices: 171 us -> 0 us
  Pallas kernels: 0 us -> 88.2 us
  matrix products: 46.4 us -> 0 us
  blocking collectives: 13.8 us -> 0 us
  between operations: 13.5 us -> 0.01 us
  other arithmetic: 2.58 us -> 0 us
    all_gather x2 -> x0, waiting for transfers between devices: 170 us -> none  [the longest x1 123 us: shards(): lax.all_gather(hidden, 'tensor', axis=2, tiled=True)]
    pallas_call x0 -> x1, Pallas kernels: none -> 88.2 us  [fused(): pl.pallas_call(ring_kernel, out_shape=jax.ShapeDtypeStruct(tokens.shape,...]
    dot_general x5 -> x0, matrix products: 46.4 us -> none  [the longest x1 14.4 us: shards(): jnp.einsum('esd,ehd->esh', arrived, up_weight, preferred_element_type=jnp...]
    all_to_all x2 -> x0, blocking collectives: 13.8 us -> none  [the longest x1 8.79 us: shards(): lax.all_to_all(packed, 'expert', split_axis=0, concat_axis=2, tiled=True)[0]]
    unnamed x2 -> x3, local copies, waits for them, and re-layouts: 0.01 us -> 4.55 us
    all_to_all x1 -> x0, local copies, waits for them, and re-layouts: 3.07 us -> none  [shards(): lax.all_to_all(packed, 'expert', split_axis=0, concat_axis=2, tiled=True)[0]]
  transfers between devices with their start and end apart: 2 -> 0, of which waited for: 2 -> 0; matrix products, arithmetic and copies ran while one was open for 1% -> 0% of each run, Pallas kernels for 0% -> 0%
where the time goes in v1:
time: 93 us; the launch traced here: 92.7 us
  Pallas kernels  88.2 us (95%)
  local copies, waits for them, and re-layouts  4.55 us (5%)
    pallas_call x1, Pallas kernels, fused(): pl.pallas_call(ring_kernel, out_shape=jax.ShapeDtypeStruct(tokens.shape,...  88.2 us
    unnamed x3, local copies, waits for them, and re-layouts  4.55 us

profile of v1, /device:TPU:0, one launch (start us, length us, event | category | flops | bytes accessed | tf_op | source)
XLA Modules:
  0.0 92.7 jit_solution(5622997608647970432)
XLA Ops:
  0.0 1.5 %copy.7.routes_ref = s32[256,2]{1,0:T(8,128)} copy(s32[256,2]{0,1:T(2,128)} %param.7) | data formatting | bytes 4096 | tf_op args[1]
  1.5 1.5 %copy.8.rw_ref = f32[256,2]{1,0:T(8,128)} copy(f32[256,2]{0,1:T(2,128)} %param.8) | data formatting | bytes 4096 | tf_op args[2]
  2.9 88.2 %shard_map.64 = bf16[128,768]{1,0:T(8,128)(2,1)} custom-call(bf16[128,768]{1,0:T(8,128)(2,1)} %tok_ref.1, s32[256,2]{1,0:T(8,128)} %copy.7.routes_ref, f32[256,2]{1,0:T(8,128)} %copy.8.rw_ref, bf16[2,1024,6144]{2,1,0:T(8,128)(2,1)} %gate_ref.1, bf16[2,1024,6144]{2,1,0:T(8,128)(2,1)} %up_ref.1, bf16[2,768,8192]{2,1,0:T(8,128)(2,1)} %down_ref.1), custom_call_target="tpu_custom_call" | custom-call | flops 19327352832 | bytes 75497472 | tf_op jit(solution)/shard_map/pallas_call | solution.py:316
  91.1 1.6 %copy.10 = bf16[128,768]{1,0:T(8,128)(2,1)} copy(bf16[128,768]{1,0:T(8,128)(2,1)} %shard_map.64) | data formatting | bytes 393216

commit v2 on v1

--- a/solution.py
+++ b/solution.py
@@ -82,7 +82,7 @@
     dl = tok_ref.shape[1]
     ul = gate_ref.shape[1]
     uh = ul // 2
-    rows = routes_ref.shape[0]
+    rows = routes_ref.shape[1]
 
     tx = t % 2
     pos = (t // 2) * (1 - tx) + (n - 1 - t // 2) * tx
@@ -117,9 +117,8 @@
         cols = pl.ds(pl.multiple_of(origin(seq) * ul, 128), ul)
         return pltpu.make_async_copy(down_ref.at[:, :, cols], dbuf.at[seq], dsem.at[seq])
 
-    for seq in range(SLOTS):
-        for cp in w_copies(seq):
-            cp.start()
+    for cp in w_copies(0):
+        cp.start()
 
     xbuf[0, pl.ds(c, 1)] = tok_ref[...].reshape(1, 2, rows // 4, dl)
 
@@ -178,7 +177,7 @@
         def body(i, carry):
             gu, e = i // 2, i % 2
             x = xbuf[seq].reshape(rows, dl)
-            r = dot_t(x, wbuf[s, gu, e, h * uh:(h + 1) * uh, :])
+            r = dot_t(wbuf[s, gu, e, h * uh:(h + 1) * uh, :], x)
             if seq == 0:
                 acc[gu, e, h] = r
             else:
@@ -200,28 +199,29 @@
         if seq + SLOTS < n:
             for cp in w_copies(seq + SLOTS):
                 cp.start()
-        if seq + SLOTS == n - 1:
-            for q in range(n):
-                d_copy(q).start()
 
     for h in range(2):
         for way in range(2):
             start(ring_copy(0, way, 1, h))
         start(sis_copy(0, 0, h))
-    gate_up(0)
+    for seq in range(1, SLOTS):
+        for cp in w_copies(seq):
+            cp.start()
     for d in range(1, half):
         for h in range(2):
             for way in range(2):
                 arrive(0, d, h, way)
-        for way in range(2):
-            gate_up(seq_of(way, d))
+            gate_up(2 * (d - 1) + h)
     for h in range(2):
         arrive(0, half, h, h)
+    gate_up(n - 2)
     for h in range(2):
         sis_wait(0, n - 1, h)
     w_wait(n - 1)
-
-    r0, r1 = routes_ref[:, 0:1], routes_ref[:, 1:2]
+    for seq in range(n):
+        d_copy(seq).start()
+
+    r0, r1 = routes_ref[0:1, :], routes_ref[1:2, :]
     mine = jnp.where(c == 0, r0, r1)
     other = jnp.where(c == 0, r1, r0)
 
@@ -253,7 +253,7 @@
                 a = hbuf[e, h]
             else:
                 a = jnp.where(r0 == 2 * c + e, sbuf[seq - 1, 0, h].astype(F32), sbuf[seq - 1, 1, h].astype(F32)).astype(BF16)
-            r = dot_t(a, dbuf[seq, e, :, h * uh:(h + 1) * uh])
+            r = jnp.dot(dbuf[seq, e, :, h * uh:(h + 1) * uh], a, preferred_element_type=F32)
             if seq == 0 and h == 0:
                 racc[e] = r
             else:
@@ -285,21 +285,22 @@
                 sis_wait(1, seq, h)
                 down(seq, h)
 
-    w0, w1 = rw_ref[:, 0:1], rw_ref[:, 1:2]
+    w0, w1 = rw_ref[0:1, :], rw_ref[1:2, :]
     zero = jnp.zeros_like(w0)
     total = None
     for e in range(2):
         f = jnp.where(r0 == 2 * c + e, w0, zero) + jnp.where(r1 == 2 * c + e, w1, zero)
         term = f * racc[e]
         total = term if total is None else total + term
-    cbuf[...] = total.reshape(2, rows // 2, dl)
+    for q in range(2):
+        cbuf[q] = total[:, q * (rows // 2):(q + 1) * (rows // 2)]
     fin = pltpu.make_async_remote_copy(
         src_ref=cbuf.at[1 - c], dst_ref=ebuf, send_sem=fin_send, recv_sem=fin_recv,
         device_id=sister, device_id_type=MESH,
     )
     start(fin)
     fin.wait_recv()
-    out_ref[...] = (cbuf[c] + ebuf[...]).astype(BF16)
+    out_ref[...] = jnp.transpose(cbuf[c] + ebuf[...]).astype(BF16)
     for cp in pending:
         cp.wait_send()
 
@@ -322,15 +323,15 @@
             pltpu.VMEM((n, 2, 2, rows // 4, dl), BF16),
             pltpu.VMEM((SLOTS, 2, 2, ul, dl), BF16),
             pltpu.VMEM((n, 2, dl, ul), BF16),
-            pltpu.VMEM((2, 2, 2, rows, uh), F32),
-            pltpu.VMEM((2, 2, rows, uh), BF16),
-            pltpu.VMEM((2, rows, uh), BF16),
-            pltpu.VMEM((2, rows, uh), BF16),
-            pltpu.VMEM((2, rows, uh), BF16),
-            pltpu.VMEM((n - 1, 2, 2, rows, uh), BF16),
-            pltpu.VMEM((2, rows, dl), F32),
-            pltpu.VMEM((2, rows // 2, dl), F32),
-            pltpu.VMEM((rows // 2, dl), F32),
+            pltpu.VMEM((2, 2, 2, uh, rows), F32),
+            pltpu.VMEM((2, 2, uh, rows), BF16),
+            pltpu.VMEM((2, uh, rows), BF16),
+            pltpu.VMEM((2, uh, rows), BF16),
+            pltpu.VMEM((2, uh, rows), BF16),
+            pltpu.VMEM((n - 1, 2, 2, uh, rows), BF16),
+            pltpu.VMEM((2, dl, rows), F32),
+            pltpu.VMEM((2, dl, rows // 2), F32),
+            pltpu.VMEM((dl, rows // 2), F32),
             dma((SLOTS, 2)), dma((n,)),
             dma((2, 2, n // 2, 2)), dma((2, 2, n // 2, 2)),
             dma((2, n, 2)), dma((2, n, 2)),
@@ -340,7 +341,7 @@
             collective_id=0, has_side_effects=True, vmem_limit_bytes=64 * 1024 * 1024 - 256 * 1024
         ),
         cost_estimate=pl.CostEstimate(flops=flops, bytes_accessed=moved, transcendentals=4 * rows * ul),
-    )(tokens, routes, route_weights, gate_weight, up_weight, down_weight)
+    )(tokens, routes.T, route_weights.T, gate_weight, up_weight, down_weight)
 
 
 def solution(mesh):

time: 93 us -> 90.8 us (0.976)
  local copies, waits for them, and re-layouts: 4.55 us -> 1.62 us
    unnamed x3 -> x1, local copies, waits for them, and re-layouts: 4.55 us -> 1.62 us
where the time goes in v2:
time: 90.8 us; the launch traced here: 90.7 us
  Pallas kernels  89.1 us (98%)
  local copies, waits for them, and re-layouts  1.62 us (2%)
    pallas_call x1, Pallas kernels, fused(): pl.pallas_call(ring_kernel, out_shape=jax.ShapeDtypeStruct(tokens.shape,...  89.1 us

profile of v2, /device:TPU:0, one launch (start us, length us, event | category | flops | bytes accessed | tf_op | source)
XLA Modules:
  0.0 90.7 jit_solution(15677433478438522134)
XLA Ops:
  0.0 89.1 %shard_map.64 = bf16[128,768]{1,0:T(8,128)(2,1)} custom-call(bf16[128,768]{1,0:T(8,128)(2,1)} %tok_ref.1, s32[2,256]{1,0:T(2,128)} %bitcast.2, f32[2,256]{1,0:T(2,128)} %bitcast.3, bf16[2,1024,6144]{2,1,0:T(8,128)(2,1)} %gate_ref.1, bf16[2,1024,6144]{2,1,0:T(8,128)(2,1)} %up_ref.1, bf16[2,768,8192]{2,1,0:T(8,128)(2,1)} %down_ref.1), custom_call_target="tpu_custom_call" | custom-call | flops 19327352832 | bytes 75497472 | tf_op jit(solution)/shard_map/pallas_call | solution.py:317
  89.1 1.6 %copy.8 = bf16[128,768]{1,0:T(8,128)(2,1)} copy(bf16[128,768]{1,0:T(8,128)(2,1)} %shard_map.64) | data formatting | bytes 393216

commit v3 on v2

--- a/solution.py
+++ b/solution.py
@@ -194,8 +194,18 @@
         for h in range(2):
             sis_wait(0, seq, h)
         w_wait(seq)
-        for h in range(2):
-            gate_up_half(seq, h)
+        s = seq % SLOTS
+
+        def body(i, carry):
+            gu, e = i // 2, i % 2
+            r = dot_t(wbuf[s, gu, e], xbuf[seq].reshape(rows, dl)).reshape(2, uh, rows)
+            if seq == 0:
+                acc[gu, e] = r
+            else:
+                acc[gu, e] += r
+            return carry
+
+        lax.fori_loop(0, 4, body, 0)
         if seq + SLOTS < n:
             for cp in w_copies(seq + SLOTS):
                 cp.start()

time: 90.8 us -> 85.1 us (0.937)
  Pallas kernels: 89.1 us -> 83.4 us
    pallas_call x1, Pallas kernels: 89.1 us -> 83.4 us  [fused(): pl.pallas_call(ring_kernel, out_shape=jax.ShapeDtypeStruct(tokens.shape,...]
where the time goes in v3:
time: 85.1 us; the launch traced here: 85 us
  Pallas kernels  83.4 us (98%)
  local copies, waits for them, and re-layouts  1.62 us (2%)
    pallas_call x1, Pallas kernels, fused(): pl.pallas_call(ring_kernel, out_shape=jax.ShapeDtypeStruct(tokens.shape,...  83.4 us

profile of v3, /device:TPU:0, one launch (start us, length us, event | category | flops | bytes accessed | tf_op | source)
XLA Modules:
  0.0 85.0 jit_solution(17640974853538060335)
XLA Ops:
  0.0 83.4 %shard_map.64 = bf16[128,768]{1,0:T(8,128)(2,1)} custom-call(bf16[128,768]{1,0:T(8,128)(2,1)} %tok_ref.1, s32[2,256]{1,0:T(2,128)} %bitcast.2, f32[2,256]{1,0:T(2,128)} %bitcast.3, bf16[2,1024,6144]{2,1,0:T(8,128)(2,1)} %gate_ref.1, bf16[2,1024,6144]{2,1,0:T(8,128)(2,1)} %up_ref.1, bf16[2,768,8192]{2,1,0:T(8,128)(2,1)} %down_ref.1), custom_call_target="tpu_custom_call" | custom-call | flops 19327352832 | bytes 75497472 | tf_op jit(solution)/shard_map/pallas_call | solution.py:327
  83.4 1.6 %copy.8 = bf16[128,768]{1,0:T(8,128)(2,1)} copy(bf16[128,768]{1,0:T(8,128)(2,1)} %shard_map.64) | data formatting | bytes 393216
